TPU v7x, 256 devices: a whole 4x4x8 slice. The times are simulated.
256 devices in a mesh: gz: 64 (over z, x, core), gy: 4 (over y).
Axes of the slice: x: 4, y: 4, z: 8, core: 2. Of those that a mesh axis runs over, the one named last changes fastest.
Arguments:
- parcel_cell: int32 [1048576], P(('gz', 'gy')), may hold values from 0 to 131071
- parcel_offset: float32 [3, 1048576], P(None, ('gz', 'gy')), may hold values from 0 to 1
- parcel_volume: float32 [1048576], P(('gz', 'gy')), may hold values from 1 to 8
- parcel_force: float32 [3, 1048576], P(None, ('gz', 'gy')), may hold values from -24 to 24
- brick_counts: int32 [64, 4], P('gz', 'gy'), may hold values from 1 to 4096, as said below
- divergence: float32 [512, 256, 256], P('gz', 'gy'), may hold values from -6 to 6
- pressure_prev: float32 [512, 256, 256], P('gz', 'gy'), may hold values from -6 to 6
- gas_density: float32 [512, 256, 256], P('gz', 'gy'), may hold values from 0.5 to 2
Outputs:
- gas_fraction: float32 [512, 256, 256], P('gz', 'gy')
- momentum_source: float32 [512, 3, 256, 256], P('gz', None, 'gy')
- pressure: float32 [512, 256, 256], P('gz', 'gy')
- residual: float32 [512, 256, 256], P('gz', 'gy')
Inputs may be any that keep to these rules, and one draw needn't show every extreme that they name: brick_counts gives the number of live parcels of each brick, held in the brick's first slots; one brick holds exactly 4096 and one exactly 1.
All inputs are finite; a program needn't handle non-finite values.
Results may differ from a plain program's by a relative error of at most 0.0021.
Values sent between devices are 32-bit elements; how exact they have to be, the bound alone decides.
No kernel may reach another device: no remote copies, remote signals or barrier semaphores. Data moves between devices by JAX's collectives and lax.ppermute only.
A program may use at most 64 MiB of HBM per device.

v0:
```python
import functools

import jax
import jax.numpy as jnp
from jax import lax
from jax.experimental import pallas as pl
from jax.experimental.pallas import tpu as pltpu
from jax.sharding import PartitionSpec as P

CZ = 8
CY = 64
CX = 256
PCAP = 4096
ITERS = 2
REACH = 5
ZE = CZ + 2 * REACH
YE = 88
LEAD = 12
LIST = PCAP // 256
TILES = CY // 8
HALF = 128
CHUNK = 256
TALL = 16

smooth_rate = 0.15
stiffness = 0.002

VMEM_LIMIT = 36 * 1024 * 1024


def chunk_values(parcels, grid_rows, row_first, shift_y):
    cell = parcels[0:1].astype(jnp.int32)
    home_z = lax.shift_right_logical(cell, 14)
    home_y = lax.shift_right_logical(cell, 8) & 63
    home_x = cell & 255
    count = parcels.shape[1]
    taps = lax.broadcasted_iota(jnp.int32, (8, count), 0).astype(jnp.float32) - 3.0

    def tap_table(offset, inside):
        distance = taps + 0.5 - offset
        weight = jnp.where(inside, jnp.exp(-0.5 * distance * distance), 0.0)
        return weight * (1.0 / jnp.sum(weight, axis=0, keepdims=True))

    seven = taps < 3.5
    place_y = taps + (home_y.astype(jnp.float32) + (row_first + shift_y))
    place_x = taps + home_x.astype(jnp.float32)
    table_z = tap_table(parcels[1:2], seven)
    table_y = tap_table(parcels[2:3], seven & (place_y >= 0.0) & (place_y < grid_rows))
    table_x = tap_table(parcels[3:4], seven & (place_x >= 0.0) & (place_x < float(CX)))
    return home_z, home_y, home_x, table_z, table_y, table_x


def axis_rows(rows, first, home, table, least=None):
    count = home.shape[1]
    lane_row = lax.broadcasted_iota(jnp.int32, (8, count), 0)
    tap_base = lane_row - (home - 3)
    tiles = []
    for tile in range(rows // 8):
        at = first + 8 * tile
        tap = tap_base + at
        fits = (tap & -8) == 0
        if least is not None:
            fits = fits & (lane_row >= least - at)
        tiles.append(jnp.take_along_axis(table, jnp.where(fits, tap, 7), axis=0))
    return tiles[0] if len(tiles) == 1 else jnp.concatenate(tiles, axis=0)


def row_of(cell):
    return lax.shift_right_logical(cell.astype(jnp.int32), 8) & 63


def count_where(condition):
    return jnp.sum(condition.astype(jnp.float32)).astype(jnp.int32)


def deposit(parcels_ref, base, row_first, grid_rows, shift_z, shift_y, planes, plane_first, window, lead, acc_first, acc_ref, lhs_ref, rhs_ref):
    rows = TALL if window is None else 8
    volume = parcels_ref[base : base + LIST, 4, :]
    begin = 0
    if shift_y == 0:
        total = count_where(volume != 0.0)
    else:
        home_row = row_of(parcels_ref[base : base + LIST, 0, :])
        if shift_y < 0:
            total = count_where(volume != 0.0)
            begin = lax.shift_right_logical(
                count_where((volume != 0.0) & (home_row < CY - 3 - REACH)), CHUNK.bit_length() - 1
            )
        else:
            total = count_where((volume != 0.0) & (home_row < 3 + REACH))

    def chunk_step(index, carry):
        start = index * CHUNK
        parcels = parcels_ref[base + index]
        home_z, home_y, home_x, table_z, table_y, table_x = chunk_values(
            parcels, grid_rows, row_first, float(shift_y)
        )
        block = 64
        for part in range(CX // block):
            weight_x = axis_rows(block, part * block, home_x, table_x)
            rhs_ref[part * block : (part + 1) * block, :] = weight_x.astype(jnp.bfloat16)
        rows_z = -(-planes // 8) * 8
        weight_z = axis_rows(rows_z, plane_first - REACH - shift_z, home_z, table_z)
        loaded = [
            weight_z * (parcels[4:5] if field == 0 else parcels[4:5] * parcels[4 + field : 5 + field])
            for field in range(4)
        ]

        def spread_window(first, least):
            weight_y = axis_rows(
                rows, first - (lead + shift_y), home_y, table_y,
                None if least is None else least - lead,
            )
            for field in range(4):
                for pair in range(planes // 2):
                    both = jnp.concatenate(
                        [
                            loaded[field][2 * pair : 2 * pair + 1] * weight_y,
                            loaded[field][2 * pair + 1 : 2 * pair + 2] * weight_y,
                        ],
                        axis=0,
                    )
                    at = (field * planes + 2 * pair) * rows
                    lhs_ref[at : at + 2 * rows, :] = both.astype(jnp.bfloat16)

        def add_window(first):
            for field in range(4):
                product = lax.dot_general(
                    lhs_ref[field * planes * rows : (field + 1) * planes * rows, :],
                    rhs_ref[...],
                    (((1,), (1,)), ((), ())),
                    preferred_element_type=jnp.float32,
                )
                for plane in range(planes):
                    for half in range(2):
                        acc_ref[field, plane_first - acc_first + plane, half, pl.ds(first, rows), :] += product[
                            plane * rows : (plane + 1) * rows, half * HALF : (half + 1) * HALF
                        ]

        if window is not None:
            spread_window(window, None)
            add_window(window)
            return carry

        slot = lax.broadcasted_iota(jnp.int32, (1, CHUNK), 1) + start
        row_home = home_y.astype(jnp.float32)
        lowest = jnp.min(jnp.where(slot < total, row_home, float(CY))).astype(jnp.int32)
        highest = jnp.max(jnp.where(slot < total, row_home, 0.0)).astype(jnp.int32)
        row_low = lowest + (lead - 3)
        row_high = highest + (lead + 4)

        def window_step(carried):
            logical = carried
            first = jnp.minimum(logical, acc_ref.shape[3] - TALL)
            spread_window(first, logical)
            add_window(first)
            return logical + TALL

        lax.while_loop(lambda carried: carried < row_high, window_step, row_low)
        return carry

    end = lax.shift_right_logical(total + (CHUNK - 1), CHUNK.bit_length() - 1)
    lax.fori_loop(begin, end, chunk_step, 0)


def sort_kernel(count_ref, cell_ref, offset_ref, volume_ref, force_ref, guess_ref, density_ref, diverge_ref, up_ref, down_ref, rows_ref, cell_held_ref, data_ref, hot_ref, prefix_ref, dest_ref, lhs_ref, total_ref, sems):
    lists = [
        pltpu.make_async_copy(cell_ref, cell_held_ref, sems.at[0]),
        pltpu.make_async_copy(offset_ref, data_ref.at[1:4], sems.at[1]),
        pltpu.make_async_copy(volume_ref, data_ref.at[4:5], sems.at[2]),
        pltpu.make_async_copy(force_ref, data_ref.at[5:8], sems.at[3]),
    ]
    edges = []
    for out_ref, upper in ((up_ref, True), (down_ref, False)):
        at = LIST
        for source, depth in ((guess_ref, 2), (density_ref, 2), (diverge_ref, 1)):
            for plane in range(depth):
                edges.append(
                    pltpu.make_async_copy(
                        source.at[CZ - depth + plane if upper else plane],
                        out_ref.at[at : at + TILES],
                        sems.at[4 + len(edges)],
                    )
                )
                at += TILES
    for part, source in enumerate((guess_ref, density_ref, diverge_ref)):
        for side in range(2):
            edges.append(
                pltpu.make_async_copy(
                    source.at[:, side * (TILES - 1)], rows_ref.at[2 * part + side], sems.at[4 + len(edges)]
                )
            )
    for copy in lists + edges:
        copy.start()
    for copy in lists:
        copy.wait()
    data_ref[0:1, :] = cell_held_ref[...].astype(jnp.float32)
    live_count = count_ref[0, 0]
    block = 256
    blocks = PCAP // block
    bins = lax.broadcasted_iota(jnp.int32, (CY, block), 0)
    slots = lax.broadcasted_iota(jnp.int32, (1, block), 1)

    def hot_of(index):
        cut = slice(index * block, (index + 1) * block)
        home_row = lax.shift_right_logical(cell_held_ref[:, cut], 8) & 63
        return (bins == home_row) & (slots + index * block < live_count)

    for index in range(blocks):
        hot_ref[index * CY : (index + 1) * CY, :] = hot_of(index).astype(jnp.float32).astype(jnp.bfloat16)
    before = lax.broadcasted_iota(jnp.int32, (block, block), 0)
    after = lax.broadcasted_iota(jnp.int32, (block, block), 1)
    upto = (before <= after).astype(jnp.float32).astype(jnp.bfloat16)
    prefix_ref[...] = jnp.dot(hot_ref[...], upto, preferred_element_type=jnp.float32)
    carry = jnp.zeros((CY, 1), jnp.float32)
    carries = []
    for index in range(blocks):
        carries.append(carry)
        carry = carry + prefix_ref[index * CY : (index + 1) * CY, block - 1 : block]
    total = jnp.broadcast_to(carry, (CY, 128))
    row = lax.broadcasted_iota(jnp.int32, (CY, 128), 0)
    summed = total
    for shift in (1, 2, 4, 8, 16, 32):
        summed = summed + jnp.where(row >= shift, pltpu.roll(summed, shift, 0), 0.0)
    first = (summed - total)[:, 0:1]
    for index in range(blocks):
        cut = slice(index * block, (index + 1) * block)
        place = prefix_ref[index * CY : (index + 1) * CY, :] + (first + carries[index])
        hot = hot_of(index)
        dest = jnp.sum(jnp.where(hot, place, 0.0), axis=0, keepdims=True) - 1.0
        dest_ref[:, cut] = dest.astype(jnp.int32)

    total_ref[...] = jnp.zeros_like(total_ref)
    width = 512

    def route(index, unused):
        start = pl.multiple_of(index * width, width)
        dest = dest_ref[:, pl.ds(start, width)]
        high = lax.shift_right_arithmetic(dest, 8)
        low = dest & 255
        data = data_ref[:, pl.ds(start, width)]
        top = data.astype(jnp.bfloat16).astype(jnp.float32)
        rest = data - top
        middle = rest.astype(jnp.bfloat16).astype(jnp.float32)
        lanes = lax.broadcasted_iota(jnp.int32, (256, width), 0)
        rhs = (lanes == low).astype(jnp.float32).astype(jnp.bfloat16)
        wide = jnp.broadcast_to(high, (8, width))
        for split, values in enumerate((top, middle, rest - middle)):
            for pair in range(8):
                both = jnp.concatenate(
                    [
                        jnp.where(wide == 2 * pair, values, 0.0),
                        jnp.where(wide == 2 * pair + 1, values, 0.0),
                    ],
                    axis=0,
                )
                at = split * 128 + pair * 16
                lhs_ref[at : at + 16, :] = both.astype(jnp.bfloat16)
        total_ref[...] += lax.dot_general(
            lhs_ref[...], rhs, (((1,), (1,)), ((), ())), preferred_element_type=jnp.float32
        )
        return unused

    steps = lax.shift_right_logical(live_count + (width - 1), 9)
    lax.fori_loop(0, steps, route, 0)
    for part in range(LIST):
        at = part * 8
        sorted_part = (
            total_ref[at : at + 8, :] + total_ref[128 + at : 136 + at, :]
        ) + total_ref[256 + at : 264 + at, :]
        up_ref[part] = sorted_part
        down_ref[part] = sorted_part
    for copy in edges:
        copy.wait()


FIELDS = ((2, 2), (2, 2), (1, 1))


def pack_kernel(sorted_ref, below_ref, above_ref, edge_ref, north_ref, south_ref):
    for out_ref in (north_ref, south_ref):
        for index, source in enumerate((sorted_ref, below_ref, above_ref)):
            out_ref[index * LIST : (index + 1) * LIST] = source[0:LIST]
        out_ref[3 * LIST + 7, 2:8, :] = jnp.zeros((6, CX), jnp.float32)
    for side, out_ref in ((1, north_ref), (0, south_ref)):
        slot = 0
        for part, (depth, wide) in enumerate(FIELDS):
            first = (0, 2, 4)[part]
            rows = slice(8 - wide, 8) if side else slice(0, wide)
            for plane in range(CZ + 2 * depth):
                if depth <= plane < CZ + depth:
                    values = edge_ref[2 * part + side, plane - depth, rows, :]
                else:
                    ref, inner = (below_ref, plane) if plane < depth else (above_ref, plane - CZ - depth)
                    values = ref[LIST + (first + inner) * TILES + side * (TILES - 1), rows, :]
                out_ref[3 * LIST + slot // 8, slot % 8 : slot % 8 + wide, :] = values
                slot += wide


def middle_deposit(list_ref, row_first, grid_rows, shift_z, planes, plane_first, acc_first, acc_ref, lhs_ref, rhs_ref):
    deposit(
        list_ref, 0, row_first, grid_rows, shift_z, 0, planes, plane_first, None, LEAD - MID.start,
        acc_first, acc_ref, lhs_ref, rhs_ref,
    )


def own_kernel(grid_rows, row_ref, parcels_ref, acc_ref, lhs_ref, rhs_ref):
    row_first = row_ref[0].astype(jnp.float32)
    acc_ref[...] = jnp.zeros_like(acc_ref)
    middle_deposit(parcels_ref, row_first, grid_rows, 0, 14, 2, 2, acc_ref, lhs_ref, rhs_ref)


def z_kernel(grid_rows, row_ref, below_ref, above_ref, acc_ref, lhs_ref, rhs_ref):
    row_first = row_ref[0].astype(jnp.float32)
    acc_ref[...] = jnp.zeros_like(acc_ref)
    middle_deposit(below_ref, row_first, grid_rows, -CZ, 8, 0, 0, acc_ref, lhs_ref, rhs_ref)
    middle_deposit(above_ref, row_first, grid_rows, CZ, 8, 10, 2, acc_ref, lhs_ref, rhs_ref)


def gather_fields(south_ref, north_ref, below_ref, above_ref, sources, targets):
    slot = 0
    for part, (own_ref, out_ref, (depth, wide)) in enumerate(zip(sources, targets, FIELDS)):
        first = (0, 2, 4)[part]
        for plane in range(CZ + 2 * depth):
            for half in range(2):
                cut = slice(half * HALF, (half + 1) * HALF)
                if depth <= plane < CZ + depth:
                    out_ref[plane, half, OWN, :] = own_ref[plane - depth, :, cut]
                else:
                    ref, inner = (below_ref, plane) if plane < depth else (above_ref, plane - CZ - depth)
                    at = LIST + (first + inner) * TILES
                    for tile in range(TILES):
                        out_ref[plane, half, LEAD + 8 * tile : LEAD + 8 * tile + 8, :] = ref[at + tile, :, cut]
                edge = 3 * LIST + slot // 8
                inner_rows = slice(slot % 8, slot % 8 + wide)
                out_ref[plane, half, LEAD - wide : LEAD, :] = south_ref[edge, inner_rows, cut]
                out_ref[plane, half, LEAD + CY : LEAD + CY + wide, :] = north_ref[edge, inner_rows, cut]
            slot += wide


def beside_y(row_first, grid_rows, south_ref, north_ref, acc_ref, lhs_ref, rhs_ref):
    for parcels_ref, shift_y, window in (
        (south_ref, -CY, LEAD - REACH),
        (north_ref, CY, LEAD + CY - 3),
    ):
        for part, (shift_z, planes, plane_first) in enumerate(((0, 14, 2), (-CZ, 8, 0), (CZ, 8, 10))):
            deposit(
                parcels_ref, LIST * part, row_first, grid_rows, shift_z, shift_y, planes, plane_first,
                window, LEAD, 0, acc_ref, lhs_ref, rhs_ref,
            )


MID = slice(8, 80)
LOW = slice(7, 79)
HIGH = slice(9, 81)
OWN = slice(LEAD, LEAD + CY)


def x_pair(left, right):
    lane = lax.broadcasted_iota(jnp.int32, left.shape, 1)
    start, stop = lane == 0, lane == HALF - 1
    left_west, right_west = pltpu.roll(left, 1, 1), pltpu.roll(right, 1, 1)
    left_east, right_east = pltpu.roll(left, HALF - 1, 1), pltpu.roll(right, HALF - 1, 1)
    return (
        jnp.where(start, 0.0, left_west) + jnp.where(stop, right_east, left_east),
        jnp.where(start, left_west, right_west) + jnp.where(stop, 0.0, right_east),
    )


def x_slope(left, right):
    lane = lax.broadcasted_iota(jnp.int32, left.shape, 1)
    start, stop = lane == 0, lane == HALF - 1
    left_west, right_west = pltpu.roll(left, 1, 1), pltpu.roll(right, 1, 1)
    left_east, right_east = pltpu.roll(left, HALF - 1, 1), pltpu.roll(right, HALF - 1, 1)
    return (
        jnp.where(stop, right_east, left_east) - jnp.where(start, 0.0, left_west),
        jnp.where(stop, 0.0, right_east) - jnp.where(start, left_west, right_west),
    )


def beside_of(ref, plane):
    centre = [ref[plane, half, MID, :] for half in range(2)]
    pairs = x_pair(*centre)
    sums = [
        (ref[plane - 1, half, MID, :] + ref[plane + 1, half, MID, :])
        + (ref[plane, half, LOW, :] + ref[plane, half, HIGH, :])
        + pairs[half]
        for half in range(2)
    ]
    return centre, sums


def field_kernel(
    grid_rows,
    row_ref,
    below_ref,
    above_ref,
    south_ref,
    north_ref,
    acc_own_ref,
    acc_z_ref,
    density_own_ref,
    guess_own_ref,
    diverge_own_ref,
    fraction_ref,
    momentum_ref,
    residual_ref,
    direction_ref,
    mapped_ref,
    scaled_own_ref,
    twice_ref,
    high_ref,
    low_ref,
    north_edge_ref,
    south_edge_ref,
    high_face_ref,
    low_face_ref,
    north_face_ref,
    south_face_ref,
    dots_ref,
    scaled_ref,
    mobility_ref,
    diagonal_ref,
    first_ref,
    second_ref,
    mob_ref,
    guess_ref,
    wide_ref,
    density_ref,
    diverge_ref,
    rate_ref,
    lhs_ref,
    rhs_ref,
    load_sems,
):
    row_first = row_ref[0].astype(jnp.float32)
    loads = [
        pltpu.make_async_copy(acc_z_ref.at[:, 0:CZ], first_ref.at[:, 0:CZ, :, MID, :], load_sems.at[0]),
        pltpu.make_async_copy(
            acc_z_ref.at[:, CZ : 2 * CZ], first_ref.at[:, CZ + 2 : ZE, :, MID, :], load_sems.at[1]
        ),
        pltpu.make_async_copy(acc_own_ref, second_ref.at[:, 2:16, :, MID, :], load_sems.at[2]),
    ]
    for load in loads:
        load.start()
    for field in range(4):
        edge = jnp.zeros((ZE, 2, 8, HALF), jnp.float32)
        first_ref[field, :, :, 0 : MID.start, :] = edge
        first_ref[field, :, :, MID.stop : YE, :] = edge
        first_ref[field, CZ : CZ + 2, :, MID, :] = jnp.zeros((2, 2, 72, HALF), jnp.float32)
    gather_fields(
        south_ref,
        north_ref,
        below_ref,
        above_ref,
        (guess_own_ref, density_own_ref, diverge_own_ref),
        (guess_ref, density_ref, diverge_ref),
    )
    loads[0].wait()
    loads[1].wait()
    beside_y(row_first, grid_rows, south_ref, north_ref, first_ref, lhs_ref, rhs_ref)
    loads[2].wait()

    def add_own(plane, carry):
        for field in range(4):
            for half in range(2):
                first_ref[field, plane, half, MID, :] += second_ref[field, plane, half, MID, :]
        return carry

    lax.fori_loop(2, 16, add_own, 0)

    row = lax.broadcasted_iota(jnp.int32, (YE, HALF), 0).astype(jnp.float32) + (row_first - LEAD)
    lane = lax.broadcasted_iota(jnp.int32, (YE, HALF), 1)
    within = (row >= 0.0) & (row < grid_rows)
    inside = within.astype(jnp.float32)
    count_y = (row >= 1.0).astype(jnp.float32) + (row < grid_rows - 1.0).astype(jnp.float32)
    for half in range(2):
        count_x = 2.0 - (lane == (0, HALF - 1)[half]).astype(jnp.float32)
        rate_ref[half] = inside * (1.0 - smooth_rate * (2.0 + count_y + count_x))
    rate_ref[2] = inside * smooth_rate
    for index, reach in enumerate((2.0, 1.0, 0.0)):
        near = within & (row >= row_first - reach) & (row < row_first + (CY + reach))
        rate_ref[3 + index] = near.astype(jnp.float32)

    for sweep, (source, target) in enumerate(
        ((first_ref, second_ref), (second_ref, first_ref), (first_ref, second_ref))
    ):

        def sweep_plane(plane, fields, source=source, target=target):
            for field in fields:
                centre, sums = beside_of(source.at[field], plane)
                for half in range(2):
                    target[field, plane, half, MID, :] = (
                        rate_ref[half, MID, :] * centre[half] + rate_ref[2, MID, :] * sums[half]
                    )

        def sweep_step(plane, carry, sweep_plane=sweep_plane):
            sweep_plane(plane, (0, 1, 2, 3))
            return carry

        sweep_plane(sweep + 1, (0, 1))
        lax.fori_loop(sweep + 2, ZE - 2 - sweep, sweep_step, 0)
        sweep_plane(ZE - 2 - sweep, (0, 1))

    filtered = second_ref

    def mobility_step(plane, carry):
        known = rate_ref[3] > 0.5
        for half in range(2):
            fraction = 1.0 / (1.0 + filtered[0, plane + 3, half])
            mobility = jnp.where(known, fraction / density_ref[plane, half], 0.0)
            mob_ref[plane, half] = mobility
            wide_ref[plane, half] = mobility * guess_ref[plane, half]
        return carry

    lax.fori_loop(0, CZ + 4, mobility_step, 0)

    def output_step(plane, carry):
        for half in range(2):
            cut = slice(half * HALF, (half + 1) * HALF)
            fraction_ref[plane, :, cut] = 1.0 / (1.0 + filtered[0, plane + REACH, half, OWN, :])
            for part in range(3):
                momentum_ref[plane, part, :, cut] = filtered[part + 1, plane + REACH, half, OWN, :]
        return carry

    lax.fori_loop(0, CZ, output_step, 0)

    direct_ref, product_ref, remain_ref = first_ref.at[0], first_ref.at[1], first_ref.at[2]

    def first_residual(plane, carry):
        at = plane + 1
        near = rate_ref[4, MID, :] > 0.5
        mobility, beside_mobility = beside_of(mob_ref, at)
        guess, beside_guess = beside_of(guess_ref, at)
        unused, beside_wide = beside_of(wide_ref, at)
        slope = x_slope(filtered[3, at + 3, 0, MID, :], filtered[3, at + 3, 1, MID, :])
        for half in range(2):
            diagonal = (3.0 + stiffness) * mobility[half] + 0.5 * beside_mobility[half]
            operated = diagonal * guess[half] - 0.5 * (
                mobility[half] * beside_guess[half] + beside_wide[half]
            )
            spread = 0.5 * (filtered[1, at + 4, half, MID, :] - filtered[1, at + 2, half, MID, :])
            spread = spread + 0.5 * (
                filtered[2, at + 3, half, HIGH, :] - filtered[2, at + 3, half, LOW, :]
            )
            spread = spread + 0.5 * slope[half]
            residual = jnp.where(near, diverge_ref[plane, half, MID, :] - spread - operated, 0.0)
            direction = jnp.where(near, residual / diagonal, 0.0)
            remain_ref[plane, half, MID, :] = residual
            direct_ref[plane, half, MID, :] = direction
            product_ref[plane, half, MID, :] = direction * mobility[half]
            diagonal_ref[plane, half, MID, :] = diagonal
            mobility_ref[plane, half, MID, :] = mobility[half]
        return carry

    lax.fori_loop(0, CZ + 2, first_residual, 0)

    scaled_ref[...] = jnp.zeros_like(scaled_ref)
    again_ref = first_ref.at[3]
    for plane in (0, CZ + 1):
        again_ref[plane] = jnp.zeros((2, YE, HALF), jnp.float32)

    def map_step(plane, sums):
        at = plane + 1
        own = rate_ref[5, MID, :] > 0.5
        directions, beside_direction = beside_of(direct_ref, at)
        unused, beside_product = beside_of(product_ref, at)
        sum_rz, sum_dw, sum_uw = sums
        for half in range(2):
            residual = jnp.where(own, remain_ref[at, half, MID, :], 0.0)
            diagonal = diagonal_ref[at, half, MID, :]
            mapped = diagonal * directions[half] - 0.5 * (
                mobility_ref[at, half, MID, :] * beside_direction[half] + beside_product[half]
            )
            mapped = jnp.where(own, mapped, 0.0)
            scaled = jnp.where(own, mapped / diagonal, 0.0)
            scaled_ref[at, half, MID, :] = scaled
            again_ref[at, half, MID, :] = scaled * mobility_ref[at, half, MID, :]
            scaled_own_ref[plane, half] = scaled[4:68]
            residual_ref[plane, half] = residual[4:68]
            direction_ref[plane, half] = directions[half][4:68]
            mapped_ref[plane, half] = mapped[4:68]
            sum_rz = sum_rz + residual * directions[half]
            sum_dw = sum_dw + directions[half] * mapped
            sum_uw = sum_uw + scaled * mapped
        return sum_rz, sum_dw, sum_uw

    zero = jnp.zeros((72, HALF), jnp.float32)
    sums = lax.fori_loop(0, CZ, map_step, (zero, zero, zero))
    for index in range(3):
        dots_ref[index] = jnp.sum(sums[index])
    def again_step(plane, total):
        at = plane + 1
        centre, beside = beside_of(scaled_ref, at)
        unused, beside_again = beside_of(again_ref, at)
        for half in range(2):
            twice = diagonal_ref[at, half, MID, :] * centre[half] - 0.5 * (
                mobility_ref[at, half, MID, :] * beside[half] + beside_again[half]
            )
            twice_ref[plane, half] = twice[4:68]
            total = total + (centre[half] * twice)[4:68]
        return total

    total = lax.fori_loop(0, CZ, again_step, jnp.zeros((CY, HALF), jnp.float32))
    dots_ref[3] = jnp.sum(total)
    high_face_ref[...] = 0.5 * (mobility_ref[CZ, :, OWN, :] + mobility_ref[CZ + 1, :, OWN, :])
    low_face_ref[...] = 0.5 * (mobility_ref[1, :, OWN, :] + mobility_ref[0, :, OWN, :])
    for face_ref, inner in ((north_face_ref, LEAD + CY - 1), (south_face_ref, LEAD - 1)):
        for plane in range(CZ):
            for half in range(2):
                face_ref[plane, half : half + 1] = 0.5 * (
                    mobility_ref[plane + 1, half, inner : inner + 1, :]
                    + mobility_ref[plane + 1, half, inner + 1 : inner + 2, :]
                )
    high_ref[...] = scaled_ref[CZ, :, OWN, :]
    low_ref[...] = scaled_ref[1, :, OWN, :]
    for plane in range(CZ):
        for half in range(2):
            north_edge_ref[plane, half : half + 1] = scaled_ref[plane + 1, half, LEAD + CY - 1 : LEAD + CY, :]
            south_edge_ref[plane, half : half + 1] = scaled_ref[plane + 1, half, LEAD : LEAD + 1, :]


def second_kernel(dots_ref, *refs):
    received, own_edges, faces, sent_ref = refs[0:4], refs[4:8], refs[8:12], refs[12]
    missing = jnp.float32(0.0)
    for got_ref, own_ref, face_ref in zip(received, own_edges, faces):
        missing = missing + jnp.sum(got_ref[...] * own_ref[...] * face_ref[...])
    values = (dots_ref[0], dots_ref[1], dots_ref[2], dots_ref[3] - missing)
    column = lax.broadcasted_iota(jnp.int32, sent_ref.shape, 1)
    sent = jnp.zeros(sent_ref.shape, jnp.float32)
    for index, value in enumerate(values):
        sent = jnp.where(column == index, value, sent)
    sent_ref[...] = sent


def final_kernel(got_ref, guess_ref, residual_ref, direction_ref, mapped_ref, scaled_ref, twice_ref, below_ref, above_ref, south_ref, north_ref, low_face_ref, high_face_ref, south_face_ref, north_face_ref, pressure_ref, final_ref):
    sums = jnp.sum(got_ref[...], axis=0, keepdims=True)
    sum_rz, sum_dw, sum_uw, sum_uv = (sums[:, index : index + 1] for index in range(4))
    step = sum_rz / sum_dw
    next_rz = sum_rz - 2.0 * step * sum_dw + step * step * sum_uw
    along = 1.0 + next_rz / sum_rz
    curvature = along * along * sum_dw - 2.0 * step * along * sum_uw + step * step * sum_uv
    next_step = next_rz / curvature
    first = step + next_step * along
    last = next_step * step

    row = lax.broadcasted_iota(jnp.int32, (CY, HALF), 0)
    for plane in range(CZ):
        for half in range(2):
            cut = slice(half * HALF, (half + 1) * HALF)
            south = south_ref[plane, half : half + 1] * south_face_ref[plane, half : half + 1]
            north = north_ref[plane, half : half + 1] * north_face_ref[plane, half : half + 1]
            past = jnp.where(row == 0, south, 0.0) + jnp.where(row == CY - 1, north, 0.0)
            if plane == 0:
                past = past + below_ref[half] * low_face_ref[half]
            if plane == CZ - 1:
                past = past + above_ref[half] * high_face_ref[half]
            twice = twice_ref[plane, half] - past
            pressure_ref[plane, :, cut] = (
                guess_ref[plane, :, cut]
                + first * direction_ref[plane, half]
                - last * scaled_ref[plane, half]
            )
            final_ref[plane, :, cut] = (
                residual_ref[plane, half] - first * mapped_ref[plane, half] + last * twice
            )


def vmem_spec():
    return pl.BlockSpec(memory_space=pltpu.VMEM)


def smem_spec():
    return pl.BlockSpec(memory_space=pltpu.SMEM)


def f32(*shape):
    return jax.ShapeDtypeStruct(shape, jnp.float32)


def params():
    return pltpu.CompilerParams(vmem_limit_bytes=VMEM_LIMIT)


def hbm_spec():
    return pl.BlockSpec(memory_space=pltpu.HBM)


def deposit_scratch():
    return [
        pltpu.VMEM((4 * 14 * TALL, CHUNK), jnp.bfloat16),
        pltpu.VMEM((CX, CHUNK), jnp.bfloat16),
    ]


def on_device(
    parcel_cell,
    parcel_offset,
    parcel_volume,
    parcel_force,
    brick_counts,
    divergence,
    pressure_prev,
    gas_density,
):
    size_z = lax.axis_size("gz")
    size_y = lax.axis_size("gy")
    grid_rows = float(size_y * CY)
    row_first = (lax.axis_index("gy") * CY).astype(jnp.int32)[None]
    up_z = [(i, (i + 1) % size_z) for i in range(size_z)]
    down_z = [((i + 1) % size_z, i) for i in range(size_z)]
    up_y = [(i, i + 1) for i in range(size_y - 1)]
    down_y = [(i + 1, i) for i in range(size_y - 1)]

    message = f32(LIST + 5 * TILES, 8, CX)
    tiled = [values.reshape(CZ, TILES, 8, CX) for values in (pressure_prev, gas_density, divergence)]
    to_up, to_down, brick_rows = pl.pallas_call(
        sort_kernel,
        out_shape=(message, message, f32(6, CZ, 8, CX)),
        in_specs=[smem_spec()] + [hbm_spec()] * 7,
        out_specs=(vmem_spec(), vmem_spec(), vmem_spec()),
        scratch_shapes=[
            pltpu.VMEM((1, PCAP), jnp.int32),
            pltpu.VMEM((8, PCAP), jnp.float32),
            pltpu.VMEM((PCAP // 256 * CY, 256), jnp.bfloat16),
            pltpu.VMEM((PCAP // 256 * CY, 256), jnp.float32),
            pltpu.VMEM((1, PCAP), jnp.int32),
            pltpu.VMEM((384, 512), jnp.bfloat16),
            pltpu.VMEM((384, 256), jnp.float32),
            pltpu.SemaphoreType.DMA((20,)),
        ],
        compiler_params=pltpu.CompilerParams(vmem_limit_bytes=60 * 1024 * 1024),
        name="order",
    )(brick_counts, parcel_cell[None], parcel_offset, parcel_volume[None], parcel_force, *tiled)
    acc_own = pl.pallas_call(
        functools.partial(own_kernel, grid_rows),
        out_shape=f32(4, 14, 2, MID.stop - MID.start, HALF),
        in_specs=[smem_spec(), vmem_spec()],
        out_specs=vmem_spec(),
        scratch_shapes=deposit_scratch(),
        compiler_params=params(),
        cost_estimate=pl.CostEstimate(flops=8_000_000_000, bytes_accessed=8_000_000, transcendentals=0),
        name="own",
    )(row_first, to_up)
    below = lax.ppermute(to_up, "gz", up_z)
    above = lax.ppermute(to_down, "gz", down_z)
    edge_rows = f32(3 * LIST + 8, 8, CX)
    to_north, to_south = pl.pallas_call(
        pack_kernel,
        out_shape=(edge_rows, edge_rows),
        in_specs=[vmem_spec()] * 4,
        out_specs=(vmem_spec(), vmem_spec()),
        compiler_params=params(),
        name="pack",
    )(to_up, below, above, brick_rows)
    south = lax.ppermute(to_north, "gy", up_y)
    north = lax.ppermute(to_south, "gy", down_y)
    acc_z = pl.pallas_call(
        functools.partial(z_kernel, grid_rows),
        out_shape=f32(4, 2 * CZ, 2, MID.stop - MID.start, HALF),
        in_specs=[smem_spec()] + [vmem_spec()] * 2,
        out_specs=vmem_spec(),
        scratch_shapes=deposit_scratch(),
        compiler_params=params(),
        cost_estimate=pl.CostEstimate(flops=8_000_000_000, bytes_accessed=8_000_000, transcendentals=0),
        name="beside_z",
    )(row_first, below, above)
    halves = f32(CZ, 2, CY, HALF)
    face_z, face_y = f32(2, CY, HALF), f32(CZ, 2, HALF)
    (
        fraction, momentum, residual, direction, mapped, scaled, twice,
        high, low, north_edge, south_edge, high_face, low_face, north_face, south_face, dots,
    ) = pl.pallas_call(
        functools.partial(field_kernel, grid_rows),
        out_shape=(f32(CZ, CY, CX), f32(CZ, 3, CY, CX))
        + (halves,) * 5
        + (face_z, face_z, face_y, face_y) * 2
        + (f32(4),),
        in_specs=[smem_spec()] + [vmem_spec()] * 4 + [pl.BlockSpec(memory_space=pl.ANY)] * 2 + [vmem_spec()] * 3,
        out_specs=tuple([vmem_spec()] * 15 + [smem_spec()]),
        scratch_shapes=[pltpu.VMEM((CZ + 2, 2, YE, HALF), jnp.float32)] * 3
        + [
            pltpu.VMEM((4, ZE, 2, YE, HALF), jnp.float32),
            pltpu.VMEM((4, ZE, 2, YE, HALF), jnp.float32),
            pltpu.VMEM((CZ + 4, 2, YE, HALF), jnp.float32),
            pltpu.VMEM((CZ + 4, 2, YE, HALF), jnp.float32),
            pltpu.VMEM((CZ + 4, 2, YE, HALF), jnp.float32),
            pltpu.VMEM((CZ + 4, 2, YE, HALF), jnp.float32),
            pltpu.VMEM((CZ + 2, 2, YE, HALF), jnp.float32),
            pltpu.VMEM((6, YE, HALF), jnp.float32),
        ]
        + deposit_scratch()
        + [pltpu.SemaphoreType.DMA((3,))],
        compiler_params=params(),
        name="fields",
    )(row_first, below, above, south, north, acc_own, acc_z, gas_density, pressure_prev, divergence)

    scaled_below = lax.ppermute(high, "gz", up_z)
    scaled_above = lax.ppermute(low, "gz", down_z)
    scaled_south = lax.ppermute(north_edge, "gy", up_y)
    scaled_north = lax.ppermute(south_edge, "gy", down_y)
    every = size_z * size_y
    received = (scaled_below, scaled_above, scaled_south, scaled_north)
    faces = (low_face, high_face, south_face, north_face)
    sent = pl.pallas_call(
        second_kernel,
        out_shape=f32(every, 128),
        in_specs=[smem_spec()] + [vmem_spec()] * 12,
        out_specs=vmem_spec(),
        compiler_params=params(),
        name="second",
    )(dots, *received, low, high, south_edge, north_edge, *faces)
    got = lax.all_to_all(sent, ("gz", "gy"), 0, 0, tiled=True)
    pressure, final = pl.pallas_call(
        final_kernel,
        out_shape=(f32(CZ, CY, CX), f32(CZ, CY, CX)),
        in_specs=[vmem_spec()] * 15,
        out_specs=(vmem_spec(), vmem_spec()),
        compiler_params=params(),
        name="final",
    )(got, pressure_prev, residual, direction, mapped, scaled, twice, *received, *faces)
    return (fraction, momentum, pressure, final)


def solution(mesh):
    return jax.shard_map(
        on_device,
        mesh=mesh,
        in_specs=(
            P(("gz", "gy")),
            P(None, ("gz", "gy")),
            P(("gz", "gy")),
            P(None, ("gz", "gy")),
            P("gz", "gy"),
            P("gz", "gy", None),
            P("gz", "gy", None),
            P("gz", "gy", None),
        ),
        out_specs=(
            P("gz", "gy", None),
            P("gz", None, "gy", None),
            P("gz", "gy", None),
            P("gz", "gy", None),
        ),
        check_vma=False,
    )
```

profile of v0, /device:TPU:1, one launch (start us, length us, event | category | flops | bytes accessed | tf_op | source)
XLA Modules:
  0.0 105.5 jit_solution(3061562325705771073)
XLA Ops:
  1.3 3.6 %order.1 = (f32[56,8,256]{2,1,0:T(8,128)}, f32[56,8,256]{2,1,0:T(8,128)}, f32[6,8,8,256]{3,2,1,0:T(8,128)}) custom-call(s32[1,1]{1,0:T(1,128)S(6)} %copy.13.count_ref, s32[1,4096]{1,0:T(1,128)} %bitcast.15, f32[3,4096]{1,0:T(4,128)} %offset_ref.1, f32[1,4096]{1,0:T(1,128)} %bitcast.16, f32[3,4096]{1,0:T(4,128)} %force_ref.1, f32[8,8,8,256]{3,2,1,0:T(8,128)} %bitcast.10, ...), custom_call_target="tpu_custom_call" | custom-call | tf_op jit(solution)/shard_map/order/pallas_call | solution.py:717
  4.8 3.0 %collective-permute-start.1 = (f32[56,8,256]{2,1,0:T(8,128)}, f32[56,8,256]{2,1,0:T(8,128)S(1)}, u32[]{:S(2)}, u32[]{:S(2)}) collective-permute-start(f32[56,8,256]{2,1,0:T(8,128)} %get-tuple-element.28), channel_id=1, source_target_pairs={{4,0},{8,4},{12,8},{16,12},{20,16},{24,20},{28,24},{32,28},{36,32}... | collective-permute-start | bytes 1376264 | tf_op jit(solution)/shard_map/ppermute | solution.py:746
  7.9 1.1 copy-done.3
  8.9 3.8 %own.1.acc_own_ref = f32[4,14,2,72,128]{4,3,2,1,0:T(8,128)S(1)} custom-call(s32[1]{0:T(128)} %bitcast.row_ref, f32[56,8,256]{2,1,0:T(8,128)S(1)} %copy-done.3), custom_call_target="tpu_custom_call" | custom-call | flops 8000000000 | bytes 8000000 | tf_op jit(solution)/shard_map/own/pallas_call | solution.py:735
  12.7 1.2 %collective-permute-done.1.above_ref = f32[56,8,256]{2,1,0:T(8,128)S(1)} collective-permute-done((f32[56,8,256]{2,1,0:T(8,128)}, f32[56,8,256]{2,1,0:T(8,128)S(1)}, u32[]{:S(2)}, u32[]{:S(2)}) %collective-permute-start.1) | collective-permute-done | bytes 458784 | tf_op jit(solution)/shard_map/ppermute | solution.py:746
  13.9 2.2 %collective-permute-done.below_ref = f32[56,8,256]{2,1,0:T(8,128)S(1)} collective-permute-done((f32[56,8,256]{2,1,0:T(8,128)}, f32[56,8,256]{2,1,0:T(8,128)S(1)}, u32[]{:S(2)}, u32[]{:S(2)}) %collective-permute-start) | collective-permute-done | bytes 458784 | tf_op jit(solution)/shard_map/ppermute | solution.py:745
  16.1 0.1 pack.1
  16.1 2.3 %collective-permute-start.2 = (f32[56,8,256]{2,1,0:T(8,128)S(1)}, f32[56,8,256]{2,1,0:T(8,128)S(1)}, u32[]{:S(2)}, u32[]{:S(2)}) collective-permute-start(f32[56,8,256]{2,1,0:T(8,128)S(1)} %get-tuple-element.30), channel_id=1, source_target_pairs={{0,1},{1,2},{2,3},{4,5},{5,6},{6,7},{8,9},{9,10},{10,11},{12,13},{... | collective-permute-start | bytes 1376264 | tf_op jit(solution)/shard_map/ppermute | solution.py:756
  18.5 0.0 copy-start
  18.5 0.0 copy-start.1
  18.5 0.0 copy-start.2
  18.5 1.4 %collective-permute-start.3 = (f32[56,8,256]{2,1,0:T(8,128)S(1)}, f32[56,8,256]{2,1,0:T(8,128)S(1)}, u32[]{:S(2)}, u32[]{:S(2)}) collective-permute-start(f32[56,8,256]{2,1,0:T(8,128)S(1)} %get-tuple-element.31), channel_id=1, source_target_pairs={{1,0},{2,1},{3,2},{5,4},{6,5},{7,6},{9,8},{10,9},{11,10},{13,12},{... | collective-permute-start | bytes 1376264 | tf_op jit(solution)/shard_map/ppermute | solution.py:757
  19.9 5.8 %beside_z.1.acc_z_ref = f32[4,16,2,72,128]{4,3,2,1,0:T(8,128)S(1)} custom-call(s32[1]{0:T(128)} %bitcast.row_ref, f32[56,8,256]{2,1,0:T(8,128)S(1)} %collective-permute-done.below_ref, f32[56,8,256]{2,1,0:T(8,128)S(1)} %collective-permute-done.1.above_ref), custom_call_target="tpu_custom_call" | custom-call | flops 8000000000 | bytes 8000000 | tf_op jit(solution)/shard_map/beside_z/pallas_call | solution.py:758
  25.7 2.2 %collective-permute-done.3.north_ref = f32[56,8,256]{2,1,0:T(8,128)S(1)} collective-permute-done((f32[56,8,256]{2,1,0:T(8,128)S(1)}, f32[56,8,256]{2,1,0:T(8,128)S(1)}, u32[]{:S(2)}, u32[]{:S(2)}) %collective-permute-start.3) | collective-permute-done | bytes 458784 | tf_op jit(solution)/shard_map/ppermute | solution.py:757
  28.0 20.9 %fields.1 = (f32[8,64,256]{2,1,0:T(8,128)}, f32[8,3,64,256]{3,2,1,0:T(8,128)}, f32[8,2,64,128]{3,2,1,0:T(8,128)S(1)}, f32[8,2,64,128]{3,2,1,0:T(8,128)S(1)}, f32...) custom-call(s32[1]{0:T(128)} %bitcast.row_ref, ...), custom_call_target="tpu_custom_call" | custom-call | tf_op jit(solution)/shard_map/fields/pallas_call | solution.py:773
  48.9 3.8 %collective-permute-start.4 = (f32[2,64,128]{2,1,0:T(8,128)S(1)}, f32[2,64,128]{2,1,0:T(8,128)S(1)}, u32[]{:S(2)}, u32[]{:S(2)}) collective-permute-start(f32[2,64,128]{2,1,0:T(8,128)S(1)} %get-tuple-element.35.refs_5_), channel_id=1, source_target_pairs={{0,4},{4,8},{8,12},{12,16},{16,20},{20,24},{24,28},{28,32},{32,36}... | collective-permute-start | bytes 196616 | tf_op jit(solution)/shard_map/ppermute | solution.py:798
  52.7 7.6 %collective-permute-start.5 = (f32[2,64,128]{2,1,0:T(8,128)S(1)}, f32[2,64,128]{2,1,0:T(8,128)S(1)}, u32[]{:S(2)}, u32[]{:S(2)}) collective-permute-start(f32[2,64,128]{2,1,0:T(8,128)S(1)} %get-tuple-element.36.refs_4_), channel_id=1, source_target_pairs={{4,0},{8,4},{12,8},{16,12},{20,16},{24,20},{28,24},{32,28},{36,32}... | collective-permute-start | bytes 196616 | tf_op jit(solution)/shard_map/ppermute | solution.py:799
  60.3 4.9 %collective-permute-start.6 = (f32[8,2,128]{2,1,0:T(2,128)S(1)}, f32[8,2,128]{2,1,0:T(2,128)S(1)}, u32[]{:S(2)}, u32[]{:S(2)}) collective-permute-start(f32[8,2,128]{2,1,0:T(2,128)S(1)} %get-tuple-element.37.refs_7_), channel_id=1, source_target_pairs={{0,1},{1,2},{2,3},{4,5},{5,6},{6,7},{8,9},{9,10},{10,11},{12,13},{... | collective-permute-start | bytes 24584 | tf_op jit(solution)/shard_map/ppermute | solution.py:800
  65.2 1.3 %collective-permute-start.7 = (f32[8,2,128]{2,1,0:T(2,128)S(1)}, f32[8,2,128]{2,1,0:T(2,128)S(1)}, u32[]{:S(2)}, u32[]{:S(2)}) collective-permute-start(f32[8,2,128]{2,1,0:T(2,128)S(1)} %get-tuple-element.38.refs_6_), channel_id=1, source_target_pairs={{1,0},{2,1},{3,2},{5,4},{6,5},{7,6},{9,8},{10,9},{11,10},{13,12},{... | collective-permute-start | bytes 24584 | tf_op jit(solution)/shard_map/ppermute | solution.py:801
  66.5 3.3 %collective-permute-done.7.refs_3_.north_ref = f32[8,2,128]{2,1,0:T(2,128)S(1)} collective-permute-done((f32[8,2,128]{2,1,0:T(2,128)S(1)}, f32[8,2,128]{2,1,0:T(2,128)S(1)}, u32[]{:S(2)}, u32[]{:S(2)}) %collective-permute-start.7) | collective-permute-done | bytes 8224 | tf_op jit(solution)/shard_map/ppermute | solution.py:801
  69.8 0.0 collective-permute-done.4.refs_0_.below_ref
  69.8 0.7 second.1
  70.5 33.6 %all_to_all.11 = f32[256,1,128]{2,1,0:T(1,128)S(1)} all-to-all(f32[256,1,128]{2,1,0:T(1,128)S(1)} %bitcast.14), channel_id=1, replica_groups=mesh['gz'=64,'gy'=4] {'gz','gy'}, dimensions={0} | all-to-all | bytes 262144 | tf_op jit(solution)/shard_map/all_to_all | solution.py:813
  104.2 1.3 %final.1 = (f32[8,64,256]{2,1,0:T(8,128)}, f32[8,64,256]{2,1,0:T(8,128)}) custom-call(f32[256,128]{1,0:T(8,128)S(1)} %bitcast.13, f32[8,64,256]{2,1,0:T(8,128)S(1)} %copy-done, f32[8,2,64,128]{3,2,1,0:T(8,128)S(1)} %get-tuple-element.43.residual_ref, f32[8,2,64,128]{3,2,1,0:T(8,128)S(1)} %get-tuple-element.44.direction_ref, ...), custom_call_target="tpu_custom_call" | custom-call | tf_op jit(solution)/shard_map/final/pallas_call | solution.py:814
  (10 shorter events, 0.0 us)
Async XLA Ops:
  4.8 9.1 %collective-permute-start.1 = (f32[56,8,256]{2,1,0:T(8,128)}, f32[56,8,256]{2,1,0:T(8,128)S(1)}, u32[]{:S(2)}, u32[]{:S(2)}) collective-permute-start(f32[56,8,256]{2,1,0:T(8,128)} %get-tuple-element.28), channel_id=1, source_target_pairs={{4,0},{8,4},{12,8},{16,12},{20,16},{24,20},{28,24},{32,28},{36,32}... | collective-permute-start | bytes 1376264 | tf_op jit(solution)/shard_map/ppermute | solution.py:746
  7.9 8.2 %collective-permute-start = (f32[56,8,256]{2,1,0:T(8,128)}, f32[56,8,256]{2,1,0:T(8,128)S(1)}, u32[]{:S(2)}, u32[]{:S(2)}) collective-permute-start(f32[56,8,256]{2,1,0:T(8,128)} %get-tuple-element.27.sorted_ref.parcels_ref), channel_id=1, source_target_pairs={{0,4},{4,8},{8,12},{12,16},{16,20},{20,24},{24,28},{28,32},{32,36}... | collective-permute-start | bytes 1376264 | tf_op jit(solution)/shard_map/ppermute | solution.py:745
  7.9 1.1 copy-start.3
  8.9 7.1 %copy-start.4 = (f32[6,8,8,256]{3,2,1,0:T(8,128)S(1)}, f32[6,8,8,256]{3,2,1,0:T(8,128)}, u32[]{:S(2)}) copy-start(f32[6,8,8,256]{3,2,1,0:T(8,128)} %get-tuple-element.29.edge_ref) | copy-start | bytes 1179652
  16.1 9.6 %collective-permute-start.2 = (f32[56,8,256]{2,1,0:T(8,128)S(1)}, f32[56,8,256]{2,1,0:T(8,128)S(1)}, u32[]{:S(2)}, u32[]{:S(2)}) collective-permute-start(f32[56,8,256]{2,1,0:T(8,128)S(1)} %get-tuple-element.30), channel_id=1, source_target_pairs={{0,1},{1,2},{2,3},{4,5},{5,6},{6,7},{8,9},{9,10},{10,11},{12,13},{... | collective-permute-start | bytes 1376264 | tf_op jit(solution)/shard_map/ppermute | solution.py:756
  18.5 9.5 %copy-start = (f32[8,64,256]{2,1,0:T(8,128)S(1)}, f32[8,64,256]{2,1,0:T(8,128)}, u32[]{:S(2)}) copy-start(f32[8,64,256]{2,1,0:T(8,128)} %guess_ref.1) | copy-start | bytes 1572868
  18.5 9.5 %copy-start.1 = (f32[8,64,256]{2,1,0:T(8,128)S(1)}, f32[8,64,256]{2,1,0:T(8,128)}, u32[]{:S(2)}) copy-start(f32[8,64,256]{2,1,0:T(8,128)} %density_own_ref.1) | copy-start | bytes 1572868
  18.5 9.5 %copy-start.2 = (f32[8,64,256]{2,1,0:T(8,128)S(1)}, f32[8,64,256]{2,1,0:T(8,128)}, u32[]{:S(2)}) copy-start(f32[8,64,256]{2,1,0:T(8,128)} %diverge_own_ref.1) | copy-start | bytes 1572868
  18.5 9.5 %collective-permute-start.3 = (f32[56,8,256]{2,1,0:T(8,128)S(1)}, f32[56,8,256]{2,1,0:T(8,128)S(1)}, u32[]{:S(2)}, u32[]{:S(2)}) collective-permute-start(f32[56,8,256]{2,1,0:T(8,128)S(1)} %get-tuple-element.31), channel_id=1, source_target_pairs={{1,0},{2,1},{3,2},{5,4},{6,5},{7,6},{9,8},{10,9},{11,10},{13,12},{... | collective-permute-start | bytes 1376264 | tf_op jit(solution)/shard_map/ppermute | solution.py:757
  48.9 20.9 %collective-permute-start.4 = (f32[2,64,128]{2,1,0:T(8,128)S(1)}, f32[2,64,128]{2,1,0:T(8,128)S(1)}, u32[]{:S(2)}, u32[]{:S(2)}) collective-permute-start(f32[2,64,128]{2,1,0:T(8,128)S(1)} %get-tuple-element.35.refs_5_), channel_id=1, source_target_pairs={{0,4},{4,8},{8,12},{12,16},{16,20},{20,24},{24,28},{28,32},{32,36}... | collective-permute-start | bytes 196616 | tf_op jit(solution)/shard_map/ppermute | solution.py:798
  52.7 17.1 %collective-permute-start.5 = (f32[2,64,128]{2,1,0:T(8,128)S(1)}, f32[2,64,128]{2,1,0:T(8,128)S(1)}, u32[]{:S(2)}, u32[]{:S(2)}) collective-permute-start(f32[2,64,128]{2,1,0:T(8,128)S(1)} %get-tuple-element.36.refs_4_), channel_id=1, source_target_pairs={{4,0},{8,4},{12,8},{16,12},{20,16},{24,20},{28,24},{32,28},{36,32}... | collective-permute-start | bytes 196616 | tf_op jit(solution)/shard_map/ppermute | solution.py:799
  60.3 6.2 %collective-permute-start.6 = (f32[8,2,128]{2,1,0:T(2,128)S(1)}, f32[8,2,128]{2,1,0:T(2,128)S(1)}, u32[]{:S(2)}, u32[]{:S(2)}) collective-permute-start(f32[8,2,128]{2,1,0:T(2,128)S(1)} %get-tuple-element.37.refs_7_), channel_id=1, source_target_pairs={{0,1},{1,2},{2,3},{4,5},{5,6},{6,7},{8,9},{9,10},{10,11},{12,13},{... | collective-permute-start | bytes 24584 | tf_op jit(solution)/shard_map/ppermute | solution.py:800
  65.2 4.6 %collective-permute-start.7 = (f32[8,2,128]{2,1,0:T(2,128)S(1)}, f32[8,2,128]{2,1,0:T(2,128)S(1)}, u32[]{:S(2)}, u32[]{:S(2)}) collective-permute-start(f32[8,2,128]{2,1,0:T(2,128)S(1)} %get-tuple-element.38.refs_6_), channel_id=1, source_target_pairs={{1,0},{2,1},{3,2},{5,4},{6,5},{7,6},{9,8},{10,9},{11,10},{13,12},{... | collective-permute-start | bytes 24584 | tf_op jit(solution)/shard_map/ppermute | solution.py:801
where the time goes:
time: 106 us
  Pallas kernels  36.2 us (34%)
  blocking collectives  33.6 us (32%)
  starting transfers between devices  24.3 us (23%)
  waiting for transfers between devices  8.83 us (8%)
  between operations  1.41 us (1%)
  local copies, waits for them, and re-layouts  1.07 us (1%)
    all_to_all x1, blocking collectives, on_device(): got = lax.all_to_all(sent, ('gz', 'gy'), 0, 0, tiled=True)  33.6 us
    pallas_call x1, Pallas kernels, on_device(): pl.pallas_call(functools.partial(field_kernel, grid_rows), out_shape=(f32...  20.9 us
    ppermute x1, starting transfers between devices, on_device(): scaled_above = lax.ppermute(low, 'gz', down_z)  7.61 us
    pallas_call x1, Pallas kernels, on_device(): pl.pallas_call(functools.partial(z_kernel, grid_rows), out_shape=f32(4, 2...  5.79 us
    ppermute x1, starting transfers between devices, on_device(): scaled_south = lax.ppermute(north_edge, 'gy', up_y)  4.87 us
    pallas_call x1, Pallas kernels, on_device(): pl.pallas_call(functools.partial(own_kernel, grid_rows), out_shape=f32(4,...  3.82 us
    ppermute x1, starting transfers between devices, on_device(): scaled_below = lax.ppermute(high, 'gz', up_z)  3.78 us
    pallas_call x1, Pallas kernels, on_device(): pl.pallas_call(sort_kernel, out_shape=(message, message, f32(6, CZ, 8, CX...  3.55 us
  transfers between devices with their start and end apart: 8, of which 4 were waited for; matrix products, arithmetic and copies ran while one was open for 0% of the time, Pallas kernels for 9%

commit v1 on v0

--- a/solution.py
+++ b/solution.py
@@ -499,7 +499,7 @@
             return carry
 
         sweep_plane(sweep + 1, (0, 1))
-        lax.fori_loop(sweep + 2, ZE - 2 - sweep, sweep_step, 0)
+        lax.fori_loop(sweep + 2, ZE - 2 - sweep, sweep_step, 0, unroll=2)
         sweep_plane(ZE - 2 - sweep, (0, 1))
 
     filtered = second_ref

time: 106 us -> 100 us (0.943); the launches traced: 106 us -> 101 us
  blocking collectives: 33.6 us -> 27.3 us
  Pallas kernels: 36.2 us -> 42.1 us
  waiting for transfers between devices: 8.83 us -> 5.43 us
    all_to_all x1, blocking collectives: 33.6 us -> 27.3 us  [on_device(): got = lax.all_to_all(sent, ('gz', 'gy'), 0, 0, tiled=True)]
    pallas_call x1, Pallas kernels: 5.79 us -> 11 us  [on_device(): pl.pallas_call(functools.partial(z_kernel, grid_rows), out_shape=f32(4, 2...]
    ppermute x1, starting transfers between devices: 3.78 us -> 0.08 us  [on_device(): scaled_below = lax.ppermute(high, 'gz', up_z)]
    ppermute x1, starting transfers between devices: 2.31 us -> 4.86 us  [on_device(): south = lax.ppermute(to_north, 'gy', up_y)]
    ppermute x1, waiting for transfers between devices: 2.24 us -> 0.01 us  [on_device(): north = lax.ppermute(to_south, 'gy', down_y)]
    ppermute x1, starting transfers between devices: 0.01 us -> 1.28 us  [on_device(): below = lax.ppermute(to_up, 'gz', up_z)]
  transfers between devices with their start and end apart: 8 -> 8, of which waited for: 4 -> 3; matrix products, arithmetic and copies ran while one was open for 0% -> 0% of each run, Pallas kernels for 9% -> 15%
where the time goes in v1:
time: 100 us; the launch traced here: 101 us
  Pallas kernels  42.1 us (42%)
  blocking collectives  27.3 us (27%)
  starting transfers between devices  23.3 us (23%)
  waiting for transfers between devices  5.43 us (5%)
  between operations  1.44 us (1%)
  local copies, waits for them, and re-layouts  1.07 us (1%)
    all_to_all x1, blocking collectives, on_device(): got = lax.all_to_all(sent, ('gz', 'gy'), 0, 0, tiled=True)  27.3 us
    pallas_call x1, Pallas kernels, on_device(): pl.pallas_call(functools.partial(field_kernel, grid_rows), out_shape=(f32...  20.4 us
    pallas_call x1, Pallas kernels, on_device(): pl.pallas_call(functools.partial(z_kernel, grid_rows), out_shape=f32(4, 2...  11 us
    ppermute x1, starting transfers between devices, on_device(): scaled_above = lax.ppermute(low, 'gz', down_z)  6.7 us
    ppermute x1, starting transfers between devices, on_device(): scaled_south = lax.ppermute(north_edge, 'gy', up_y)  4.95 us
    ppermute x1, starting transfers between devices, on_device(): south = lax.ppermute(to_north, 'gy', up_y)  4.86 us
    pallas_call x1, Pallas kernels, on_device(): pl.pallas_call(functools.partial(own_kernel, grid_rows), out_shape=f32(4,...  4.44 us
    pallas_call x1, Pallas kernels, on_device(): pl.pallas_call(sort_kernel, out_shape=(message, message, f32(6, CZ, 8, CX...  4.17 us
  transfers between devices with their start and end apart: 8, of which 3 were waited for; matrix products, arithmetic and copies ran while one was open for 0% of the time, Pallas kernels for 15%

profile of v1, /device:TPU:1, one launch (start us, length us, event | category | flops | bytes accessed | tf_op | source)
XLA Modules:
  0.0 100.7 jit_solution(481491879752714480)
XLA Ops:
  1.3 4.2 %order.1 = (f32[56,8,256]{2,1,0:T(8,128)}, f32[56,8,256]{2,1,0:T(8,128)}, f32[6,8,8,256]{3,2,1,0:T(8,128)}) custom-call(s32[1,1]{1,0:T(1,128)S(6)} %copy.13.count_ref, s32[1,4096]{1,0:T(1,128)} %bitcast.15, f32[3,4096]{1,0:T(4,128)} %offset_ref.1, f32[1,4096]{1,0:T(1,128)} %bitcast.16, f32[3,4096]{1,0:T(4,128)} %force_ref.1, f32[8,8,8,256]{3,2,1,0:T(8,128)} %bitcast.10, ...), custom_call_target="tpu_custom_call" | custom-call | tf_op jit(solution)/shard_map/order/pallas_call | solution.py:717
  5.5 2.7 %collective-permute-start.1 = (f32[56,8,256]{2,1,0:T(8,128)}, f32[56,8,256]{2,1,0:T(8,128)S(1)}, u32[]{:S(2)}, u32[]{:S(2)}) collective-permute-start(f32[56,8,256]{2,1,0:T(8,128)} %get-tuple-element.28), channel_id=1, source_target_pairs={{4,0},{8,4},{12,8},{16,12},{20,16},{24,20},{28,24},{32,28},{36,32}... | collective-permute-start | bytes 1376264 | tf_op jit(solution)/shard_map/ppermute | solution.py:746
  8.2 1.3 %collective-permute-start = (f32[56,8,256]{2,1,0:T(8,128)}, f32[56,8,256]{2,1,0:T(8,128)S(1)}, u32[]{:S(2)}, u32[]{:S(2)}) collective-permute-start(f32[56,8,256]{2,1,0:T(8,128)} %get-tuple-element.27.sorted_ref.parcels_ref), channel_id=1, source_target_pairs={{0,4},{4,8},{8,12},{12,16},{16,20},{20,24},{24,28},{28,32},{32,36}... | collective-permute-start | bytes 1376264 | tf_op jit(solution)/shard_map/ppermute | solution.py:745
  9.4 1.1 %copy-done.3 = f32[56,8,256]{2,1,0:T(8,128)S(1)} copy-done((f32[56,8,256]{2,1,0:T(8,128)S(1)}, f32[56,8,256]{2,1,0:T(8,128)}, u32[]{:S(2)}) %copy-start.3) | copy-done | bytes 458776
  10.5 4.4 %own.1.acc_own_ref = f32[4,14,2,72,128]{4,3,2,1,0:T(8,128)S(1)} custom-call(s32[1]{0:T(128)} %bitcast.row_ref, f32[56,8,256]{2,1,0:T(8,128)S(1)} %copy-done.3), custom_call_target="tpu_custom_call" | custom-call | flops 8000000000 | bytes 8000000 | tf_op jit(solution)/shard_map/own/pallas_call | solution.py:735
  14.9 0.8 collective-permute-done.1.above_ref
  15.7 1.5 %collective-permute-done.below_ref = f32[56,8,256]{2,1,0:T(8,128)S(1)} collective-permute-done((f32[56,8,256]{2,1,0:T(8,128)}, f32[56,8,256]{2,1,0:T(8,128)S(1)}, u32[]{:S(2)}, u32[]{:S(2)}) %collective-permute-start) | collective-permute-done | bytes 458784 | tf_op jit(solution)/shard_map/ppermute | solution.py:745
  17.3 0.1 pack.1
  17.4 4.9 %collective-permute-start.2 = (f32[56,8,256]{2,1,0:T(8,128)S(1)}, f32[56,8,256]{2,1,0:T(8,128)S(1)}, u32[]{:S(2)}, u32[]{:S(2)}) collective-permute-start(f32[56,8,256]{2,1,0:T(8,128)S(1)} %get-tuple-element.30), channel_id=1, source_target_pairs={{0,1},{1,2},{2,3},{4,5},{5,6},{6,7},{8,9},{9,10},{10,11},{12,13},{... | collective-permute-start | bytes 1376264 | tf_op jit(solution)/shard_map/ppermute | solution.py:756
  22.2 0.0 copy-start
  22.3 0.0 copy-start.1
  22.3 0.0 copy-start.2
  22.3 1.4 %collective-permute-start.3 = (f32[56,8,256]{2,1,0:T(8,128)S(1)}, f32[56,8,256]{2,1,0:T(8,128)S(1)}, u32[]{:S(2)}, u32[]{:S(2)}) collective-permute-start(f32[56,8,256]{2,1,0:T(8,128)S(1)} %get-tuple-element.31), channel_id=1, source_target_pairs={{1,0},{2,1},{3,2},{5,4},{6,5},{7,6},{9,8},{10,9},{11,10},{13,12},{... | collective-permute-start | bytes 1376264 | tf_op jit(solution)/shard_map/ppermute | solution.py:757
  23.7 11.0 %beside_z.1.acc_z_ref = f32[4,16,2,72,128]{4,3,2,1,0:T(8,128)S(1)} custom-call(s32[1]{0:T(128)} %bitcast.row_ref, f32[56,8,256]{2,1,0:T(8,128)S(1)} %collective-permute-done.below_ref, f32[56,8,256]{2,1,0:T(8,128)S(1)} %collective-permute-done.1.above_ref), custom_call_target="tpu_custom_call" | custom-call | flops 8000000000 | bytes 8000000 | tf_op jit(solution)/shard_map/beside_z/pallas_call | solution.py:758
  34.7 0.0 collective-permute-done.2.south_ref
  34.7 20.4 %fields.1 = (f32[8,64,256]{2,1,0:T(8,128)}, f32[8,3,64,256]{3,2,1,0:T(8,128)}, f32[8,2,64,128]{3,2,1,0:T(8,128)S(1)}, f32[8,2,64,128]{3,2,1,0:T(8,128)S(1)}, f32...) custom-call(s32[1]{0:T(128)} %bitcast.row_ref, ...), custom_call_target="tpu_custom_call" | custom-call | tf_op jit(solution)/shard_map/fields/pallas_call | solution.py:773
  55.1 0.1 collective-permute-start.4
  55.2 6.7 %collective-permute-start.5 = (f32[2,64,128]{2,1,0:T(8,128)S(1)}, f32[2,64,128]{2,1,0:T(8,128)S(1)}, u32[]{:S(2)}, u32[]{:S(2)}) collective-permute-start(f32[2,64,128]{2,1,0:T(8,128)S(1)} %get-tuple-element.36.refs_4_), channel_id=1, source_target_pairs={{4,0},{8,4},{12,8},{16,12},{20,16},{24,20},{28,24},{32,28},{36,32}... | collective-permute-start | bytes 196616 | tf_op jit(solution)/shard_map/ppermute | solution.py:799
  61.9 4.9 %collective-permute-start.6 = (f32[8,2,128]{2,1,0:T(2,128)S(1)}, f32[8,2,128]{2,1,0:T(2,128)S(1)}, u32[]{:S(2)}, u32[]{:S(2)}) collective-permute-start(f32[8,2,128]{2,1,0:T(2,128)S(1)} %get-tuple-element.37.refs_7_), channel_id=1, source_target_pairs={{0,1},{1,2},{2,3},{4,5},{5,6},{6,7},{8,9},{9,10},{10,11},{12,13},{... | collective-permute-start | bytes 24584 | tf_op jit(solution)/shard_map/ppermute | solution.py:800
  66.9 1.3 %collective-permute-start.7 = (f32[8,2,128]{2,1,0:T(2,128)S(1)}, f32[8,2,128]{2,1,0:T(2,128)S(1)}, u32[]{:S(2)}, u32[]{:S(2)}) collective-permute-start(f32[8,2,128]{2,1,0:T(2,128)S(1)} %get-tuple-element.38.refs_6_), channel_id=1, source_target_pairs={{1,0},{2,1},{3,2},{5,4},{6,5},{7,6},{9,8},{10,9},{11,10},{13,12},{... | collective-permute-start | bytes 24584 | tf_op jit(solution)/shard_map/ppermute | solution.py:801
  68.2 3.1 %collective-permute-done.7.refs_3_.north_ref = f32[8,2,128]{2,1,0:T(2,128)S(1)} collective-permute-done((f32[8,2,128]{2,1,0:T(2,128)S(1)}, f32[8,2,128]{2,1,0:T(2,128)S(1)}, u32[]{:S(2)}, u32[]{:S(2)}) %collective-permute-start.7) | collective-permute-done | bytes 8224 | tf_op jit(solution)/shard_map/ppermute | solution.py:801
  71.3 0.7 second.1
  72.0 27.3 %all_to_all.11 = f32[256,1,128]{2,1,0:T(1,128)S(1)} all-to-all(f32[256,1,128]{2,1,0:T(1,128)S(1)} %bitcast.14), channel_id=1, replica_groups=mesh['gz'=64,'gy'=4] {'gz','gy'}, dimensions={0} | all-to-all | bytes 262144 | tf_op jit(solution)/shard_map/all_to_all | solution.py:813
  99.3 1.3 %final.1 = (f32[8,64,256]{2,1,0:T(8,128)}, f32[8,64,256]{2,1,0:T(8,128)}) custom-call(f32[256,128]{1,0:T(8,128)S(1)} %bitcast.13, f32[8,64,256]{2,1,0:T(8,128)S(1)} %copy-done, f32[8,2,64,128]{3,2,1,0:T(8,128)S(1)} %get-tuple-element.43.residual_ref, f32[8,2,64,128]{3,2,1,0:T(8,128)S(1)} %get-tuple-element.44.direction_ref, ...), custom_call_target="tpu_custom_call" | custom-call | tf_op jit(solution)/shard_map/final/pallas_call | solution.py:814
  (10 shorter events, 0.0 us)
Async XLA Ops:
  5.5 10.3 %collective-permute-start.1 = (f32[56,8,256]{2,1,0:T(8,128)}, f32[56,8,256]{2,1,0:T(8,128)S(1)}, u32[]{:S(2)}, u32[]{:S(2)}) collective-permute-start(f32[56,8,256]{2,1,0:T(8,128)} %get-tuple-element.28), channel_id=1, source_target_pairs={{4,0},{8,4},{12,8},{16,12},{20,16},{24,20},{28,24},{32,28},{36,32}... | collective-permute-start | bytes 1376264 | tf_op jit(solution)/shard_map/ppermute | solution.py:746
  8.2 9.1 %collective-permute-start = (f32[56,8,256]{2,1,0:T(8,128)}, f32[56,8,256]{2,1,0:T(8,128)S(1)}, u32[]{:S(2)}, u32[]{:S(2)}) collective-permute-start(f32[56,8,256]{2,1,0:T(8,128)} %get-tuple-element.27.sorted_ref.parcels_ref), channel_id=1, source_target_pairs={{0,4},{4,8},{8,12},{12,16},{16,20},{20,24},{24,28},{28,32},{32,36}... | collective-permute-start | bytes 1376264 | tf_op jit(solution)/shard_map/ppermute | solution.py:745
  9.4 1.1 %copy-start.3 = (f32[56,8,256]{2,1,0:T(8,128)S(1)}, f32[56,8,256]{2,1,0:T(8,128)}, u32[]{:S(2)}) copy-start(f32[56,8,256]{2,1,0:T(8,128)} %get-tuple-element.27.sorted_ref.parcels_ref) | copy-start | bytes 1376260
  10.5 6.8 %copy-start.4 = (f32[6,8,8,256]{3,2,1,0:T(8,128)S(1)}, f32[6,8,8,256]{3,2,1,0:T(8,128)}, u32[]{:S(2)}) copy-start(f32[6,8,8,256]{3,2,1,0:T(8,128)} %get-tuple-element.29.edge_ref) | copy-start | bytes 1179652
  17.4 17.3 %collective-permute-start.2 = (f32[56,8,256]{2,1,0:T(8,128)S(1)}, f32[56,8,256]{2,1,0:T(8,128)S(1)}, u32[]{:S(2)}, u32[]{:S(2)}) collective-permute-start(f32[56,8,256]{2,1,0:T(8,128)S(1)} %get-tuple-element.30), channel_id=1, source_target_pairs={{0,1},{1,2},{2,3},{4,5},{5,6},{6,7},{8,9},{9,10},{10,11},{12,13},{... | collective-permute-start | bytes 1376264 | tf_op jit(solution)/shard_map/ppermute | solution.py:756
  22.2 12.5 %copy-start = (f32[8,64,256]{2,1,0:T(8,128)S(1)}, f32[8,64,256]{2,1,0:T(8,128)}, u32[]{:S(2)}) copy-start(f32[8,64,256]{2,1,0:T(8,128)} %guess_ref.1) | copy-start | bytes 1572868
  22.3 12.5 %copy-start.1 = (f32[8,64,256]{2,1,0:T(8,128)S(1)}, f32[8,64,256]{2,1,0:T(8,128)}, u32[]{:S(2)}) copy-start(f32[8,64,256]{2,1,0:T(8,128)} %density_own_ref.1) | copy-start | bytes 1572868
  22.3 12.5 %copy-start.2 = (f32[8,64,256]{2,1,0:T(8,128)S(1)}, f32[8,64,256]{2,1,0:T(8,128)}, u32[]{:S(2)}) copy-start(f32[8,64,256]{2,1,0:T(8,128)} %diverge_own_ref.1) | copy-start | bytes 1572868
  22.3 12.4 %collective-permute-start.3 = (f32[56,8,256]{2,1,0:T(8,128)S(1)}, f32[56,8,256]{2,1,0:T(8,128)S(1)}, u32[]{:S(2)}, u32[]{:S(2)}) collective-permute-start(f32[56,8,256]{2,1,0:T(8,128)S(1)} %get-tuple-element.31), channel_id=1, source_target_pairs={{1,0},{2,1},{3,2},{5,4},{6,5},{7,6},{9,8},{10,9},{11,10},{13,12},{... | collective-permute-start | bytes 1376264 | tf_op jit(solution)/shard_map/ppermute | solution.py:757
  55.1 16.2 %collective-permute-start.4 = (f32[2,64,128]{2,1,0:T(8,128)S(1)}, f32[2,64,128]{2,1,0:T(8,128)S(1)}, u32[]{:S(2)}, u32[]{:S(2)}) collective-permute-start(f32[2,64,128]{2,1,0:T(8,128)S(1)} %get-tuple-element.35.refs_5_), channel_id=1, source_target_pairs={{0,4},{4,8},{8,12},{12,16},{16,20},{20,24},{24,28},{28,32},{32,36}... | collective-permute-start | bytes 196616 | tf_op jit(solution)/shard_map/ppermute | solution.py:798
  55.2 16.1 %collective-permute-start.5 = (f32[2,64,128]{2,1,0:T(8,128)S(1)}, f32[2,64,128]{2,1,0:T(8,128)S(1)}, u32[]{:S(2)}, u32[]{:S(2)}) collective-permute-start(f32[2,64,128]{2,1,0:T(8,128)S(1)} %get-tuple-element.36.refs_4_), channel_id=1, source_target_pairs={{4,0},{8,4},{12,8},{16,12},{20,16},{24,20},{28,24},{32,28},{36,32}... | collective-permute-start | bytes 196616 | tf_op jit(solution)/shard_map/ppermute | solution.py:799
  61.9 6.3 %collective-permute-start.6 = (f32[8,2,128]{2,1,0:T(2,128)S(1)}, f32[8,2,128]{2,1,0:T(2,128)S(1)}, u32[]{:S(2)}, u32[]{:S(2)}) collective-permute-start(f32[8,2,128]{2,1,0:T(2,128)S(1)} %get-tuple-element.37.refs_7_), channel_id=1, source_target_pairs={{0,1},{1,2},{2,3},{4,5},{5,6},{6,7},{8,9},{9,10},{10,11},{12,13},{... | collective-permute-start | bytes 24584 | tf_op jit(solution)/shard_map/ppermute | solution.py:800
  66.9 4.4 %collective-permute-start.7 = (f32[8,2,128]{2,1,0:T(2,128)S(1)}, f32[8,2,128]{2,1,0:T(2,128)S(1)}, u32[]{:S(2)}, u32[]{:S(2)}) collective-permute-start(f32[8,2,128]{2,1,0:T(2,128)S(1)} %get-tuple-element.38.refs_6_), channel_id=1, source_target_pairs={{1,0},{2,1},{3,2},{5,4},{6,5},{7,6},{9,8},{10,9},{11,10},{13,12},{... | collective-permute-start | bytes 24584 | tf_op jit(solution)/shard_map/ppermute | solution.py:801

commit v2 on v1

--- a/solution.py
+++ b/solution.py
@@ -467,7 +467,7 @@
                 first_ref[field, plane, half, MID, :] += second_ref[field, plane, half, MID, :]
         return carry
 
-    lax.fori_loop(2, 16, add_own, 0)
+    lax.fori_loop(2, 16, add_own, 0, unroll=2)
 
     row = lax.broadcasted_iota(jnp.int32, (YE, HALF), 0).astype(jnp.float32) + (row_first - LEAD)
     lane = lax.broadcasted_iota(jnp.int32, (YE, HALF), 1)
@@ -513,7 +513,7 @@
             wide_ref[plane, half] = mobility * guess_ref[plane, half]
         return carry
 
-    lax.fori_loop(0, CZ + 4, mobility_step, 0)
+    lax.fori_loop(0, CZ + 4, mobility_step, 0, unroll=2)
 
     def output_step(plane, carry):
         for half in range(2):
@@ -553,7 +553,7 @@
             mobility_ref[plane, half, MID, :] = mobility[half]
         return carry
 
-    lax.fori_loop(0, CZ + 2, first_residual, 0)
+    lax.fori_loop(0, CZ + 2, first_residual, 0, unroll=2)
 
     scaled_ref[...] = jnp.zeros_like(scaled_ref)
     again_ref = first_ref.at[3]
@@ -586,7 +586,7 @@
         return sum_rz, sum_dw, sum_uw
 
     zero = jnp.zeros((72, HALF), jnp.float32)
-    sums = lax.fori_loop(0, CZ, map_step, (zero, zero, zero))
+    sums = lax.fori_loop(0, CZ, map_step, (zero, zero, zero), unroll=2)
     for index in range(3):
         dots_ref[index] = jnp.sum(sums[index])
     def again_step(plane, total):
@@ -601,7 +601,7 @@
             total = total + (centre[half] * twice)[4:68]
         return total
 
-    total = lax.fori_loop(0, CZ, again_step, jnp.zeros((CY, HALF), jnp.float32))
+    total = lax.fori_loop(0, CZ, again_step, jnp.zeros((CY, HALF), jnp.float32), unroll=2)
     dots_ref[3] = jnp.sum(total)
     high_face_ref[...] = 0.5 * (mobility_ref[CZ, :, OWN, :] + mobility_ref[CZ + 1, :, OWN, :])
     low_face_ref[...] = 0.5 * (mobility_ref[1, :, OWN, :] + mobility_ref[0, :, OWN, :])

time: 100 us -> 102 us (1.020)
  starting transfers between devices: 23.3 us -> 24.4 us
    ppermute x1, starting transfers between devices: 0.08 us -> 9.54 us  [on_device(): scaled_below = lax.ppermute(high, 'gz', up_z)]
    pallas_call x1, Pallas kernels: 11 us -> 6.7 us  [on_device(): pl.pallas_call(functools.partial(z_kernel, grid_rows), out_shape=f32(4, 2...]
    pallas_call x1, Pallas kernels: 4.44 us -> 8.48 us  [on_device(): pl.pallas_call(functools.partial(own_kernel, grid_rows), out_shape=f32(4,...]
    ppermute x1, starting transfers between devices: 4.95 us -> 1.28 us  [on_device(): scaled_south = lax.ppermute(north_edge, 'gy', up_y)]
    ppermute x1, starting transfers between devices: 4.86 us -> 1.32 us  [on_device(): south = lax.ppermute(to_north, 'gy', up_y)]
    ppermute x1, waiting for transfers between devices: 1.54 us -> 0.01 us  [on_device(): below = lax.ppermute(to_up, 'gz', up_z)]
    ppermute x1, starting transfers between devices: 2.71 us -> 1.49 us  [on_device(): above = lax.ppermute(to_down, 'gz', down_z)]
    pallas_call x1, Pallas kernels: 4.17 us -> 5.39 us  [on_device(): pl.pallas_call(sort_kernel, out_shape=(message, message, f32(6, CZ, 8, CX...]
  transfers between devices with their start and end apart: 8 -> 8, of which waited for: 3 -> 2; matrix products, arithmetic and copies ran while one was open for 0% -> 0% of each run, Pallas kernels for 15% -> 15%
where the time goes in v2:
time: 102 us
  Pallas kernels  42.2 us (41%)
  blocking collectives  28.1 us (28%)
  starting transfers between devices  24.4 us (24%)
  waiting for transfers between devices  4.6 us (5%)
  between operations  1.43 us (1%)
  local copies, waits for them, and re-layouts  1.07 us (1%)
    all_to_all x1, blocking collectives, on_device(): got = lax.all_to_all(sent, ('gz', 'gy'), 0, 0, tiled=True)  28.1 us
    pallas_call x1, Pallas kernels, on_device(): pl.pallas_call(functools.partial(field_kernel, grid_rows), out_shape=(f32...  19.5 us
    ppermute x1, starting transfers between devices, on_device(): scaled_below = lax.ppermute(high, 'gz', up_z)  9.54 us
    pallas_call x1, Pallas kernels, on_device(): pl.pallas_call(functools.partial(own_kernel, grid_rows), out_shape=f32(4,...  8.48 us
    ppermute x1, starting transfers between devices, on_device(): scaled_above = lax.ppermute(low, 'gz', down_z)  7.71 us
    pallas_call x1, Pallas kernels, on_device(): pl.pallas_call(functools.partial(z_kernel, grid_rows), out_shape=f32(4, 2...  6.7 us
    pallas_call x1, Pallas kernels, on_device(): pl.pallas_call(sort_kernel, out_shape=(message, message, f32(6, CZ, 8, CX...  5.39 us
    ppermute x1, waiting for transfers between devices, on_device(): scaled_north = lax.ppermute(south_edge, 'gy', down_y)  3.38 us
  transfers between devices with their start and end apart: 8, of which 2 were waited for; matrix products, arithmetic and copies ran while one was open for 0% of the time, Pallas kernels for 15%

profile of v2, /device:TPU:1, one launch (start us, length us, event | category | flops | bytes accessed | tf_op | source)
XLA Modules:
  0.0 101.8 jit_solution(11593860899077408746)
XLA Ops:
  1.3 5.4 %order.1 = (f32[56,8,256]{2,1,0:T(8,128)}, f32[56,8,256]{2,1,0:T(8,128)}, f32[6,8,8,256]{3,2,1,0:T(8,128)}) custom-call(s32[1,1]{1,0:T(1,128)S(6)} %copy.13.count_ref, s32[1,4096]{1,0:T(1,128)} %bitcast.15, f32[3,4096]{1,0:T(4,128)} %offset_ref.1, f32[1,4096]{1,0:T(1,128)} %bitcast.16, f32[3,4096]{1,0:T(4,128)} %force_ref.1, f32[8,8,8,256]{3,2,1,0:T(8,128)} %bitcast.10, ...), custom_call_target="tpu_custom_call" | custom-call | tf_op jit(solution)/shard_map/order/pallas_call | solution.py:717
  6.7 1.5 %collective-permute-start.1 = (f32[56,8,256]{2,1,0:T(8,128)}, f32[56,8,256]{2,1,0:T(8,128)S(1)}, u32[]{:S(2)}, u32[]{:S(2)}) collective-permute-start(f32[56,8,256]{2,1,0:T(8,128)} %get-tuple-element.28), channel_id=1, source_target_pairs={{4,0},{8,4},{12,8},{16,12},{20,16},{24,20},{28,24},{32,28},{36,32}... | collective-permute-start | bytes 1376264 | tf_op jit(solution)/shard_map/ppermute | solution.py:746
  8.2 0.3 collective-permute-start
  8.5 1.1 %copy-done.3 = f32[56,8,256]{2,1,0:T(8,128)S(1)} copy-done((f32[56,8,256]{2,1,0:T(8,128)S(1)}, f32[56,8,256]{2,1,0:T(8,128)}, u32[]{:S(2)}) %copy-start.3) | copy-done | bytes 458776
  9.6 8.5 %own.1.acc_own_ref = f32[4,14,2,72,128]{4,3,2,1,0:T(8,128)S(1)} custom-call(s32[1]{0:T(128)} %bitcast.row_ref, f32[56,8,256]{2,1,0:T(8,128)S(1)} %copy-done.3), custom_call_target="tpu_custom_call" | custom-call | flops 8000000000 | bytes 8000000 | tf_op jit(solution)/shard_map/own/pallas_call | solution.py:735
  18.0 0.0 collective-permute-done.1.above_ref
  18.1 0.1 pack.1
  18.2 1.3 %collective-permute-start.2 = (f32[56,8,256]{2,1,0:T(8,128)S(1)}, f32[56,8,256]{2,1,0:T(8,128)S(1)}, u32[]{:S(2)}, u32[]{:S(2)}) collective-permute-start(f32[56,8,256]{2,1,0:T(8,128)S(1)} %get-tuple-element.30), channel_id=1, source_target_pairs={{0,1},{1,2},{2,3},{4,5},{5,6},{6,7},{8,9},{9,10},{10,11},{12,13},{... | collective-permute-start | bytes 1376264 | tf_op jit(solution)/shard_map/ppermute | solution.py:756
  19.5 0.0 copy-start
  19.5 0.0 copy-start.1
  19.5 0.0 copy-start.2
  19.5 1.4 %collective-permute-start.3 = (f32[56,8,256]{2,1,0:T(8,128)S(1)}, f32[56,8,256]{2,1,0:T(8,128)S(1)}, u32[]{:S(2)}, u32[]{:S(2)}) collective-permute-start(f32[56,8,256]{2,1,0:T(8,128)S(1)} %get-tuple-element.31), channel_id=1, source_target_pairs={{1,0},{2,1},{3,2},{5,4},{6,5},{7,6},{9,8},{10,9},{11,10},{13,12},{... | collective-permute-start | bytes 1376264 | tf_op jit(solution)/shard_map/ppermute | solution.py:757
  21.0 6.7 %beside_z.1.acc_z_ref = f32[4,16,2,72,128]{4,3,2,1,0:T(8,128)S(1)} custom-call(s32[1]{0:T(128)} %bitcast.row_ref, f32[56,8,256]{2,1,0:T(8,128)S(1)} %collective-permute-done.below_ref, f32[56,8,256]{2,1,0:T(8,128)S(1)} %collective-permute-done.1.above_ref), custom_call_target="tpu_custom_call" | custom-call | flops 8000000000 | bytes 8000000 | tf_op jit(solution)/shard_map/beside_z/pallas_call | solution.py:758
  27.7 0.0 collective-permute-done.2.south_ref
  27.7 1.2 %collective-permute-done.3.north_ref = f32[56,8,256]{2,1,0:T(8,128)S(1)} collective-permute-done((f32[56,8,256]{2,1,0:T(8,128)S(1)}, f32[56,8,256]{2,1,0:T(8,128)S(1)}, u32[]{:S(2)}, u32[]{:S(2)}) %collective-permute-start.3) | collective-permute-done | bytes 458784 | tf_op jit(solution)/shard_map/ppermute | solution.py:757
  28.9 19.5 %fields.1 = (f32[8,64,256]{2,1,0:T(8,128)}, f32[8,3,64,256]{3,2,1,0:T(8,128)}, f32[8,2,64,128]{3,2,1,0:T(8,128)S(1)}, f32[8,2,64,128]{3,2,1,0:T(8,128)S(1)}, f32...) custom-call(s32[1]{0:T(128)} %bitcast.row_ref, ...), custom_call_target="tpu_custom_call" | custom-call | tf_op jit(solution)/shard_map/fields/pallas_call | solution.py:773
  48.4 9.5 %collective-permute-start.4 = (f32[2,64,128]{2,1,0:T(8,128)S(1)}, f32[2,64,128]{2,1,0:T(8,128)S(1)}, u32[]{:S(2)}, u32[]{:S(2)}) collective-permute-start(f32[2,64,128]{2,1,0:T(8,128)S(1)} %get-tuple-element.35.refs_5_), channel_id=1, source_target_pairs={{0,4},{4,8},{8,12},{12,16},{16,20},{20,24},{24,28},{28,32},{32,36}... | collective-permute-start | bytes 196616 | tf_op jit(solution)/shard_map/ppermute | solution.py:798
  57.9 7.7 %collective-permute-start.5 = (f32[2,64,128]{2,1,0:T(8,128)S(1)}, f32[2,64,128]{2,1,0:T(8,128)S(1)}, u32[]{:S(2)}, u32[]{:S(2)}) collective-permute-start(f32[2,64,128]{2,1,0:T(8,128)S(1)} %get-tuple-element.36.refs_4_), channel_id=1, source_target_pairs={{4,0},{8,4},{12,8},{16,12},{20,16},{24,20},{28,24},{32,28},{36,32}... | collective-permute-start | bytes 196616 | tf_op jit(solution)/shard_map/ppermute | solution.py:799
  65.6 1.3 %collective-permute-start.6 = (f32[8,2,128]{2,1,0:T(2,128)S(1)}, f32[8,2,128]{2,1,0:T(2,128)S(1)}, u32[]{:S(2)}, u32[]{:S(2)}) collective-permute-start(f32[8,2,128]{2,1,0:T(2,128)S(1)} %get-tuple-element.37.refs_7_), channel_id=1, source_target_pairs={{0,1},{1,2},{2,3},{4,5},{5,6},{6,7},{8,9},{9,10},{10,11},{12,13},{... | collective-permute-start | bytes 24584 | tf_op jit(solution)/shard_map/ppermute | solution.py:800
  66.9 1.3 %collective-permute-start.7 = (f32[8,2,128]{2,1,0:T(2,128)S(1)}, f32[8,2,128]{2,1,0:T(2,128)S(1)}, u32[]{:S(2)}, u32[]{:S(2)}) collective-permute-start(f32[8,2,128]{2,1,0:T(2,128)S(1)} %get-tuple-element.38.refs_6_), channel_id=1, source_target_pairs={{1,0},{2,1},{3,2},{5,4},{6,5},{7,6},{9,8},{10,9},{11,10},{13,12},{... | collective-permute-start | bytes 24584 | tf_op jit(solution)/shard_map/ppermute | solution.py:801
  68.2 3.4 %collective-permute-done.7.refs_3_.north_ref = f32[8,2,128]{2,1,0:T(2,128)S(1)} collective-permute-done((f32[8,2,128]{2,1,0:T(2,128)S(1)}, f32[8,2,128]{2,1,0:T(2,128)S(1)}, u32[]{:S(2)}, u32[]{:S(2)}) %collective-permute-start.7) | collective-permute-done | bytes 8224 | tf_op jit(solution)/shard_map/ppermute | solution.py:801
  71.6 0.7 second.1
  72.3 28.1 %all_to_all.11 = f32[256,1,128]{2,1,0:T(1,128)S(1)} all-to-all(f32[256,1,128]{2,1,0:T(1,128)S(1)} %bitcast.14), channel_id=1, replica_groups=mesh['gz'=64,'gy'=4] {'gz','gy'}, dimensions={0} | all-to-all | bytes 262144 | tf_op jit(solution)/shard_map/all_to_all | solution.py:813
  100.5 1.3 %final.1 = (f32[8,64,256]{2,1,0:T(8,128)}, f32[8,64,256]{2,1,0:T(8,128)}) custom-call(f32[256,128]{1,0:T(8,128)S(1)} %bitcast.13, f32[8,64,256]{2,1,0:T(8,128)S(1)} %copy-done, f32[8,2,64,128]{3,2,1,0:T(8,128)S(1)} %get-tuple-element.43.residual_ref, f32[8,2,64,128]{3,2,1,0:T(8,128)S(1)} %get-tuple-element.44.direction_ref, ...), custom_call_target="tpu_custom_call" | custom-call | tf_op jit(solution)/shard_map/final/pallas_call | solution.py:814
  (10 shorter events, 0.0 us)
Async XLA Ops:
  6.7 11.4 %collective-permute-start.1 = (f32[56,8,256]{2,1,0:T(8,128)}, f32[56,8,256]{2,1,0:T(8,128)S(1)}, u32[]{:S(2)}, u32[]{:S(2)}) collective-permute-start(f32[56,8,256]{2,1,0:T(8,128)} %get-tuple-element.28), channel_id=1, source_target_pairs={{4,0},{8,4},{12,8},{16,12},{20,16},{24,20},{28,24},{32,28},{36,32}... | collective-permute-start | bytes 1376264 | tf_op jit(solution)/shard_map/ppermute | solution.py:746
  8.2 9.9 %collective-permute-start = (f32[56,8,256]{2,1,0:T(8,128)}, f32[56,8,256]{2,1,0:T(8,128)S(1)}, u32[]{:S(2)}, u32[]{:S(2)}) collective-permute-start(f32[56,8,256]{2,1,0:T(8,128)} %get-tuple-element.27.sorted_ref.parcels_ref), channel_id=1, source_target_pairs={{0,4},{4,8},{8,12},{12,16},{16,20},{20,24},{24,28},{28,32},{32,36}... | collective-permute-start | bytes 1376264 | tf_op jit(solution)/shard_map/ppermute | solution.py:745
  8.5 1.1 %copy-start.3 = (f32[56,8,256]{2,1,0:T(8,128)S(1)}, f32[56,8,256]{2,1,0:T(8,128)}, u32[]{:S(2)}) copy-start(f32[56,8,256]{2,1,0:T(8,128)} %get-tuple-element.27.sorted_ref.parcels_ref) | copy-start | bytes 1376260
  9.6 8.5 %copy-start.4 = (f32[6,8,8,256]{3,2,1,0:T(8,128)S(1)}, f32[6,8,8,256]{3,2,1,0:T(8,128)}, u32[]{:S(2)}) copy-start(f32[6,8,8,256]{3,2,1,0:T(8,128)} %get-tuple-element.29.edge_ref) | copy-start | bytes 1179652
  18.2 9.5 %collective-permute-start.2 = (f32[56,8,256]{2,1,0:T(8,128)S(1)}, f32[56,8,256]{2,1,0:T(8,128)S(1)}, u32[]{:S(2)}, u32[]{:S(2)}) collective-permute-start(f32[56,8,256]{2,1,0:T(8,128)S(1)} %get-tuple-element.30), channel_id=1, source_target_pairs={{0,1},{1,2},{2,3},{4,5},{5,6},{6,7},{8,9},{9,10},{10,11},{12,13},{... | collective-permute-start | bytes 1376264 | tf_op jit(solution)/shard_map/ppermute | solution.py:756
  19.5 9.4 %copy-start = (f32[8,64,256]{2,1,0:T(8,128)S(1)}, f32[8,64,256]{2,1,0:T(8,128)}, u32[]{:S(2)}) copy-start(f32[8,64,256]{2,1,0:T(8,128)} %guess_ref.1) | copy-start | bytes 1572868
  19.5 9.4 %copy-start.1 = (f32[8,64,256]{2,1,0:T(8,128)S(1)}, f32[8,64,256]{2,1,0:T(8,128)}, u32[]{:S(2)}) copy-start(f32[8,64,256]{2,1,0:T(8,128)} %density_own_ref.1) | copy-start | bytes 1572868
  19.5 9.4 %copy-start.2 = (f32[8,64,256]{2,1,0:T(8,128)S(1)}, f32[8,64,256]{2,1,0:T(8,128)}, u32[]{:S(2)}) copy-start(f32[8,64,256]{2,1,0:T(8,128)} %diverge_own_ref.1) | copy-start | bytes 1572868
  19.5 9.4 %collective-permute-start.3 = (f32[56,8,256]{2,1,0:T(8,128)S(1)}, f32[56,8,256]{2,1,0:T(8,128)S(1)}, u32[]{:S(2)}, u32[]{:S(2)}) collective-permute-start(f32[56,8,256]{2,1,0:T(8,128)S(1)} %get-tuple-element.31), channel_id=1, source_target_pairs={{1,0},{2,1},{3,2},{5,4},{6,5},{7,6},{9,8},{10,9},{11,10},{13,12},{... | collective-permute-start | bytes 1376264 | tf_op jit(solution)/shard_map/ppermute | solution.py:757
  48.4 23.2 %collective-permute-start.4 = (f32[2,64,128]{2,1,0:T(8,128)S(1)}, f32[2,64,128]{2,1,0:T(8,128)S(1)}, u32[]{:S(2)}, u32[]{:S(2)}) collective-permute-start(f32[2,64,128]{2,1,0:T(8,128)S(1)} %get-tuple-element.35.refs_5_), channel_id=1, source_target_pairs={{0,4},{4,8},{8,12},{12,16},{16,20},{20,24},{24,28},{28,32},{32,36}... | collective-permute-start | bytes 196616 | tf_op jit(solution)/shard_map/ppermute | solution.py:798
  57.9 13.7 %collective-permute-start.5 = (f32[2,64,128]{2,1,0:T(8,128)S(1)}, f32[2,64,128]{2,1,0:T(8,128)S(1)}, u32[]{:S(2)}, u32[]{:S(2)}) collective-permute-start(f32[2,64,128]{2,1,0:T(8,128)S(1)} %get-tuple-element.36.refs_4_), channel_id=1, source_target_pairs={{4,0},{8,4},{12,8},{16,12},{20,16},{24,20},{28,24},{32,28},{36,32}... | collective-permute-start | bytes 196616 | tf_op jit(solution)/shard_map/ppermute | solution.py:799
  65.6 2.6 %collective-permute-start.6 = (f32[8,2,128]{2,1,0:T(2,128)S(1)}, f32[8,2,128]{2,1,0:T(2,128)S(1)}, u32[]{:S(2)}, u32[]{:S(2)}) collective-permute-start(f32[8,2,128]{2,1,0:T(2,128)S(1)} %get-tuple-element.37.refs_7_), channel_id=1, source_target_pairs={{0,1},{1,2},{2,3},{4,5},{5,6},{6,7},{8,9},{9,10},{10,11},{12,13},{... | collective-permute-start | bytes 24584 | tf_op jit(solution)/shard_map/ppermute | solution.py:800
  66.9 4.7 %collective-permute-start.7 = (f32[8,2,128]{2,1,0:T(2,128)S(1)}, f32[8,2,128]{2,1,0:T(2,128)S(1)}, u32[]{:S(2)}, u32[]{:S(2)}) collective-permute-start(f32[8,2,128]{2,1,0:T(2,128)S(1)} %get-tuple-element.38.refs_6_), channel_id=1, source_target_pairs={{1,0},{2,1},{3,2},{5,4},{6,5},{7,6},{9,8},{10,9},{11,10},{13,12},{... | collective-permute-start | bytes 24584 | tf_op jit(solution)/shard_map/ppermute | solution.py:801
